TPU v7x, 32 devices: a whole 2x2x4 slice. The times are simulated.
32 devices in a mesh: grp: 4 (over y, core), blk: 8 (over z, x).
Axes of the slice: x: 2, y: 2, z: 4, core: 2. Of those that a mesh axis runs over, the one named last changes fastest.
Arguments:
- hidden_in: bfloat16 [8, 512, 1024], P('blk', 'grp'), may hold values from -6 to 6
- attn_gain: float32 [1024], replicated, may hold values from 0.1 to 1.9
- qkv_weight: bfloat16 [1024, 3, 16, 64], P(None, None, 'grp'), may hold values from -0.09375 to 0.09375
- rel_bias: float32 [32, 16], P(None, 'grp'), may hold values from -4 to 4
- prefix_cache: bfloat16 [8, 256, 2, 16, 64], P('blk', None, None, 'grp'), may hold values from -34 to 34
- prefix_owner: int32 [8], replicated, may hold values from 0 to 7, each once
- req_prefix: int32 [8, 2], replicated, may hold values from 0 to 7
- req_pages: int32 [8, 2], replicated, may hold values from 1 to 12, 16 in all within a row
- page_table: int32 [8, 16], replicated, may hold values from 0 to 15, each once within a row
- proj_weight: bfloat16 [1024, 1024], replicated, may hold values from -0.1875 to 0.1875
- mlp_gain: float32 [1024], replicated, may hold values from 0.1 to 1.9
- in_weight: bfloat16 [1024, 4096], P(None, 'grp'), may hold values from -0.1875 to 0.1875
- out_weight: bfloat16 [4096, 1024], P('grp'), may hold values from -0.09375 to 0.09375
Outputs:
- hidden_out: bfloat16 [8, 512, 1024], P('blk', 'grp')
- suffix_cache: bfloat16 [8, 512, 2, 16, 64], P('blk', None, None, 'grp')
Inputs may be any that keep to these rules, and one draw needn't show every extreme that they name: Prefix p's keys and values are row prefix_owner[p] of prefix_cache; every owner column holds one prefix. `req_pages`: each row sums to 16 and no entry exceeds 12. `page_table`: each row is a permutation of the logical pages of a column.
All inputs are finite; a program needn't handle non-finite values.
Results may differ from a plain program's by a relative error of at most 0.012.
Values may be sent and summed in bfloat16 or wider, within the bound.
A program may use at most 128 MiB of HBM per device.

v0:
```python
import jax
import jax.numpy as jnp
from jax import lax
from jax.sharding import PartitionSpec as P

PAGE = 32
EPSILON = 1e-06
THRESHOLDS = (12, 16, 23, 32, 46, 64, 91)


def rms_scale(values, gain):
    mean_sq = jnp.mean(values * values, axis=-1, keepdims=True)
    return values * lax.rsqrt(mean_sq + EPSILON) * gain


def bucket_of(relative):
    magnitude = jnp.abs(relative)
    steps_up = jnp.zeros(relative.shape, jnp.int32)
    for limit in THRESHOLDS:
        steps_up = steps_up + (magnitude >= limit).astype(jnp.int32)
    bucket = jnp.where(magnitude < 8, magnitude, jnp.minimum(8 + steps_up, 15))
    return bucket + 16 * (relative > 0).astype(jnp.int32)


def token_meta(pages_row, lengths_row, page_size, prefix_len):
    inclusive = jnp.cumsum(lengths_row, dtype=jnp.int32)
    exclusive = inclusive - lengths_row
    request = jnp.sum(
        (pages_row[:, None] >= inclusive[None, :]).astype(jnp.int32), axis=1, dtype=jnp.int32
    )
    slot_ids = jnp.arange(lengths_row.shape[0], dtype=jnp.int32)
    start = jnp.sum(
        jnp.where(request[:, None] == slot_ids[None, :], exclusive[None, :], 0),
        axis=1,
        dtype=jnp.int32,
    )
    offsets = (pages_row - start) * page_size + prefix_len
    within = jnp.arange(page_size, dtype=jnp.int32)
    positions = (offsets[:, None] + within[None, :]).reshape(-1)
    requests = jnp.broadcast_to(request[:, None], (request.shape[0], page_size)).reshape(-1)
    return (requests, positions)


def attend_block(queries, key_rows, value_rows, query_req, query_pos, key_req, key_pos, rel_bias):
    scores = jnp.einsum("qhd,khd->hqk", queries, key_rows, preferred_element_type=jnp.float32)
    bucket = bucket_of(key_pos[None, :] - query_pos[:, None])
    bias_add = jnp.zeros(scores.shape, jnp.float32)
    for bucket_id in range(rel_bias.shape[0]):
        bias_add = jnp.where(
            (bucket == bucket_id)[None], rel_bias[bucket_id][:, None, None], bias_add
        )
    allowed = (key_req[None, :] == query_req[:, None])[None]
    scores = jnp.where(allowed, scores + bias_add, -1e30)
    row_max = jnp.max(scores, axis=-1, keepdims=True)
    weights = jnp.exp(scores - row_max)
    weights = (weights / jnp.sum(weights, axis=-1, keepdims=True)).astype(jnp.bfloat16)
    return jnp.einsum(
        "hqk,khd->qhd", weights, value_rows, preferred_element_type=jnp.float32
    ).astype(jnp.bfloat16)


def shards(
    hidden_in,
    attn_gain,
    qkv_weight,
    rel_bias,
    prefix_cache,
    prefix_owner,
    req_prefix,
    req_pages,
    page_table,
    proj_weight,
    mlp_gain,
    in_weight,
    out_weight,
):
    width = hidden_in.shape[2]
    heads_dev = qkv_weight.shape[2]
    head_dim = qkv_weight.shape[3]
    inner = heads_dev * head_dim
    residual = hidden_in[0].astype(jnp.float32)
    normed = rms_scale(residual, attn_gain).astype(jnp.bfloat16)
    qkv_flat = qkv_weight.reshape(width, 3 * inner)
    projected = jnp.dot(
        lax.all_gather(normed, "grp", axis=0, tiled=True),
        qkv_flat,
        preferred_element_type=jnp.float32,
    ).astype(jnp.bfloat16)
    column_tok = projected.shape[0]
    projected = projected.reshape(column_tok, 3, heads_dev, head_dim)
    suffix_cache = projected[:, 1:3][None]
    column = lax.axis_index("blk")
    requests_col = req_prefix.shape[1]
    prefix_ids = jnp.arange(prefix_owner.shape[0], dtype=jnp.int32)
    owner_cols = jnp.sum(
        jnp.where(
            req_prefix[:, :, None] == prefix_ids[None, None, :], prefix_owner[None, None, :], 0
        ),
        axis=2,
        dtype=jnp.int32,
    )
    my_cols = lax.dynamic_index_in_dim(owner_cols, column, 0, keepdims=False)
    prefix_len = prefix_cache.shape[1]
    slot_width = 2 * inner
    local_slot = prefix_cache.reshape(prefix_len, slot_width)
    gathered = lax.all_gather(local_slot[None], "blk", axis=0, tiled=True)
    prefix_rows = jnp.take(gathered, my_cols, axis=0)
    prefix_rows = prefix_rows.reshape(requests_col * prefix_len, 2, heads_dev, head_dim)
    key_rows = jnp.concatenate([prefix_rows[:, 0], projected[:, 1]], axis=0)
    value_rows = jnp.concatenate([prefix_rows[:, 1], projected[:, 2]], axis=0)
    pages_row = lax.dynamic_index_in_dim(page_table, column, 0, keepdims=False)
    lengths_row = lax.dynamic_index_in_dim(req_pages, column, 0, keepdims=False)
    query_req, query_pos = token_meta(pages_row, lengths_row, PAGE, prefix_len)
    slot_ids = jnp.arange(requests_col, dtype=jnp.int32)
    key_req = jnp.concatenate([jnp.repeat(slot_ids, prefix_len), query_req])
    key_pos = jnp.concatenate(
        [jnp.tile(jnp.arange(prefix_len, dtype=jnp.int32), requests_col), query_pos]
    )
    block_rows = min(512, column_tok)
    block_count = column_tok // block_rows

    def one_block(operands):
        block_q, block_req, block_pos = operands
        return attend_block(
            block_q, key_rows, value_rows, block_req, block_pos, key_req, key_pos, rel_bias
        )

    attended = lax.map(
        one_block,
        (
            projected[:, 0].reshape(block_count, block_rows, heads_dev, head_dim),
            query_req.reshape(block_count, block_rows),
            query_pos.reshape(block_count, block_rows),
        ),
    )
    attended = attended.reshape(1, column_tok, inner)
    token_heads = lax.all_to_all(attended, "grp", split_axis=1, concat_axis=2, tiled=True)[0]
    mixed = residual + jnp.dot(token_heads, proj_weight, preferred_element_type=jnp.float32)
    normed_mlp = rms_scale(mixed, mlp_gain).astype(jnp.bfloat16)
    activated = jax.nn.relu(
        jnp.dot(
            lax.all_gather(normed_mlp, "grp", axis=0, tiled=True),
            in_weight,
            preferred_element_type=jnp.float32,
        )
    ).astype(jnp.bfloat16)
    summed = lax.psum_scatter(
        jnp.dot(activated, out_weight, preferred_element_type=jnp.float32).astype(jnp.bfloat16),
        "grp",
        scatter_dimension=0,
        tiled=True,
    ).astype(jnp.float32)
    hidden_out = (mixed + summed).astype(jnp.bfloat16)[None]
    return (hidden_out, suffix_cache)


def solution(mesh):
    return jax.shard_map(
        shards,
        mesh=mesh,
        in_specs=(
            P("blk", "grp", None),
            P(),
            P(None, None, "grp", None),
            P(None, "grp"),
            P("blk", None, None, "grp", None),
            P(),
            P(),
            P(),
            P(),
            P(),
            P(),
            P(None, "grp"),
            P("grp", None),
        ),
        out_specs=(P("blk", "grp", None), P("blk", None, None, "grp", None)),
        check_vma=False,
    )
```

profile of v0, /device:TPU:0, one launch (start us, length us, event | category | flops | bytes accessed | tf_op | source)
XLA Modules:
  0.0 208.7 jit_solution(3867273368891614869)
XLA Ops:
  7.2 1.2 fusion.11
  8.5 1.8 fusion.13
  10.3 1.8 copy.46
  14.0 1.9 slice_reduce_fusion.31
  15.9 1.6 slice_reduce_fusion.30
  19.7 1.2 broadcast_compare_fusion.32
  20.9 17.4 %broadcast_compare_fusion.25 = (pred[512,1024]{1,0:T(8,128)(4,1)}, pred[512,1024]{1,0:T(8,128)(4,1)}, pred[512,1024]{1,0:T(8,128)(4,1)}, pred[512,1024]{1,0:T(8,...) fusion(s32[512]{0:T(512)S(1)} %add.896, ...), kind=kLoop, calls=%fused_computation.47 | loop fusion | flops 31981568 | bytes 16783360 | tf_op jit(solution)/shard_map/while/body/eval_jaxpr/eq | solution.py:50
  38.3 3.7 %convolution_convert_fusion.1 = bf16[512,768]{1,0:T(8,128)(2,1)} fusion(bf16[512,1024]{1,0:T(8,128)(2,1)} %all-gather.6.cloned.1.call-done, bf16[1024,768]{0,1:T(8,128)(2,1)} %bitcast.76), kind=kOutput, calls=%fused_computation.19 | convolution fusion | flops 805699584 | bytes 3407872 | tf_op jit(solution)/shard_map/dot_general | solution.py:84
  42.1 1.4 copy.48
  44.3 37.0 %all-gather.4.cloned.1.call-done = bf16[8,256,512]{2,1,0:T(8,128)(2,1)} async-done(((bf16[1,256,512]{2,1,0:T(8,128)(2,1)}), bf16[8,256,512]{2,1,0:T(8,128)(2,1)}) %all-gather.4.cloned.1.call-update) | async-done | bytes 2097168 | tf_op jit(solution)/shard_map/all_gather | solution.py:106
  81.3 2.2 %gather_fusion = bf16[2,256,512]{2,1,0:T(8,128)(2,1)S(1)} fusion(bf16[8,256,512]{2,1,0:T(8,128)(2,1)} %all-gather.4.cloned.1.call-done, s32[1024]{0:T(1024)S(1)} %pad_clamp_fusion), kind=kCustom, calls=%fused_computation | custom fusion | bytes 1048584 | tf_op jit(solution)/shard_map/jit(_take)/gather | solution.py:107
  84.6 1.4 gather.7
  86.1 29.9 %add_select_fusion = f32[4,512,1024]{2,1,0:T(8,128)} fusion(f32[4]{0:T(128)S(1)} %get-tuple-element.62, f32[4]{0:T(128)S(1)} %get-tuple-element.63, f32[4]{0:T(128)S(1)} %get-tuple-element.23, f32[4]{0:T(128)S(1)} %get-tuple-element.24, f32[4]{0:T(128)S(1)} %get-tuple-element.25, f32[4]{0:T(128)S(1)} %get-tuple-element.26, f32[4]{0:T(128)S(1)} %get-tuple-element.27, ...), kind=kOutput, calls=%fused_computation.4 | convolution fusion | flops 340787200 | bytes 26492928 | tf_op jit(solution)/shard_map/while/body/eval_jaxpr/qhd,khd->hqk/dot_general | solution.py:45
  116.0 7.5 %fusion.30 = f32[4,512]{1,0:T(4,128)S(1)} fusion(f32[4,512,1024]{2,1,0:T(8,128)} %add_select_fusion), kind=kOutput, calls=%fused_computation.138 | output fusion | flops 4195327 | bytes 8396800 | tf_op jit(solution)/shard_map/while/body/eval_jaxpr/sub | solution.py:55
  123.5 10.5 %fusion.10 = bf16[4,64,512]{2,1,0:T(8,128)(2,1)} fusion(f32[4,512]{1,0:T(4,128)S(1)} %fusion.30, bf16[512,4,64]{0,2,1:T(8,128)(2,1)S(1)} %copy-done.1, bf16[512,4,64]{0,2,1:T(8,128)(2,1)S(1)} %get-tuple-element.66, f32[4,512,1024]{2,1,0:T(8,128)} %add_select_fusion), kind=kOutput, calls=%fused_computation.21 | convolution fusion | flops 275909632 | bytes 9183232 | tf_op jit(solution)/shard_map/while/body/eval_jaxpr/hqk,khd->qhd/dot_general | solution.py:57
  134.0 1.3 copy.50
  135.8 2.9 %reduce.67 = bf16[512,256]{1,0:T(8,128)(2,1)} reduce(bf16[512,1,256]{2,1,0:T(2,128)(2,1)S(1)} %bitcast.69, bf16[]{:T(256)} %broadcast.2960), dimensions={1}, to_apply=%bitcast.52.reduce_sub_computation | reduce | bytes 524290
  139.8 9.1 %all_to_all.15 = bf16[4,2,16384]{2,1,0:T(2,128)(2,1)} all-to-all(bf16[4,2,16384]{2,1,0:T(2,128)(2,1)S(1)} %reshape.1101), channel_id=1, replica_groups=mesh['grp'=4,'blk'=8] {'grp'}, dimensions={0} | all-to-all | bytes 524288 | tf_op jit(solution)/shard_map/all_to_all | solution.py:137
  150.8 1.8 copy.51
  152.6 2.2 %multiply_reduce_fusion = (f32[128]{0:T(128)S(1)}, f32[128,1024]{1,0:T(8,128)S(1)}) fusion(bf16[128,1024]{0,1:T(8,128)(2,1)} %bitcast.71, bf16[1024,1024]{1,0:T(8,128)(2,1)} %param.22, bf16[1,128,1024]{2,1,0:T(8,128)(2,1)} %param.13), kind=kOutput, calls=%fused_computation.69 | convolution fusion | flops 268959616 | bytes 3146240 | tf_op jit(solution)/shard_map/dot_general | solution.py:138
  155.7 14.4 %all-gather.8.cloned.1.call-done = bf16[512,1024]{1,0:T(8,128)(2,1)} async-done(((bf16[128,1024]{1,0:T(8,128)(2,1)}), bf16[512,1024]{1,0:T(8,128)(2,1)}) %all-gather.8.cloned.1.call-update) | async-done | bytes 1048592 | tf_op jit(solution)/shard_map/all_gather | solution.py:142
  170.1 5.2 %convolution_convert_fusion = bf16[512,1024]{1,0:T(8,128)(2,1)} fusion(bf16[1024,1024]{1,0:T(8,128)(2,1)S(1)} %copy-done, bf16[512,1024]{1,0:T(8,128)(2,1)} %all-gather.8.cloned.1.call-done, bf16[1024,1024]{1,0:T(8,128)(2,1)} %param.24), kind=kOutput, calls=%fused_computation.18 | convolution fusion | flops 2149056512 | bytes 6291456 | tf_op jit(solution)/shard_map/dot_general | solution.py:148
  176.2 24.2 %reduce-scatter.2.cloned.1.call-done = bf16[128,1024]{1,0:T(8,128)(2,1)} async-done(((bf16[512,1024]{1,0:T(8,128)(2,1)}), bf16[128,1024]{1,0:T(8,128)(2,1)}) %reduce-scatter.2.cloned.1.call-update) | async-done | bytes 262160 | tf_op jit(solution)/shard_map/reduce_scatter | solution.py:147
  200.4 1.7 fusion.20
  (51 shorter events, 11.5 us)
Async XLA Ops:
  7.2 163.0 %copy-start = (bf16[1024,1024]{1,0:T(8,128)(2,1)S(1)}, bf16[1024,1024]{1,0:T(8,128)(2,1)}, u32[]{:S(2)}) copy-start(bf16[1024,1024]{1,0:T(8,128)(2,1)} %param.25) | copy-start | bytes 6291460
  7.2 31.1 %all-gather.6.cloned.1.call-start = ((), (), s32[]{:S(2)}) async-start(), calls=%async_computation.3 | async-start | bytes 1310720 | tf_op jit(solution)/shard_map/all_gather | solution.py:85
  10.3 71.0 %all-gather.4.cloned.1.call-start = ((), (), s32[]{:S(2)}) async-start(), calls=%async_computation.2 | async-start | bytes 2359296 | tf_op jit(solution)/shard_map/all_gather | solution.py:106
  12.2 158.0 %all-gather.8.cloned.1.call-start = ((), (), s32[]{:S(2)}) async-start(), calls=%async_computation.4 | async-start | bytes 1310720 | tf_op jit(solution)/shard_map/all_gather | solution.py:142
  116.0 7.5 %copy-start.1 = (bf16[512,4,64]{0,2,1:T(8,128)(2,1)S(1)}, bf16[512,4,64]{0,2,1:T(8,128)(2,1)}, u32[]{:S(2)}) copy-start(bf16[512,4,64]{0,2,1:T(8,128)(2,1)} %get-tuple-element.64) | copy-start | bytes 786436
  150.1 4.8 %copy-start.2 = (f32[1024]{0:T(1024)S(1)}, f32[1024]{0:T(1024)}, u32[]{:S(2)}) copy-start(f32[1024]{0:T(1024)} %param.23) | copy-start | bytes 12292
  155.7 44.8 %reduce-scatter.2.cloned.1.call-start = ((), (), s32[]{:S(2)}) async-start(), calls=%async_computation.5 | async-start | bytes 1310720 | tf_op jit(solution)/shard_map/reduce_scatter | solution.py:147
Sparse Core Ops, SparseCore 0:
  10.4 19.4 all-gather.5
  32.0 49.2 all-gather.3
  155.8 14.2 all-gather.7
  175.5 24.8 reduce-scatter.1
where the time goes:
time: 209 us
  waiting for transfers between devices  75.7 us (36%)
  matrix products  51.6 us (25%)
  other arithmetic  36.6 us (18%)
  local copies, waits for them, and re-layouts  21.6 us (10%)
  between operations  13.9 us (7%)
  blocking collectives  9.1 us (4%)
    all_gather x1, waiting for transfers between devices, shards(): gathered = lax.all_gather(local_slot[None], 'blk', axis=0, tiled=True)  37 us
    dot_general x1, matrix products, attend_block(): jnp.einsum('qhd,khd->hqk', queries, key_rows, preferred_element_type=jnp....  29.9 us
    reduce_scatter x1, waiting for transfers between devices, shards(): lax.psum_scatter(jnp.dot(activated, out_weight, preferred_element_type=jn...  24.2 us
    eq x1, other arithmetic, attend_block(): bucket == bucket_id  17.4 us
    all_gather x1, waiting for transfers between devices, shards(): lax.all_gather(normed_mlp, 'grp', axis=0, tiled=True)  14.4 us
    dot_general x1, matrix products, attend_block(): jnp.einsum('hqk,khd->qhd', weights, value_rows, preferred_element_type=jn...  10.5 us
    all_to_all x1, blocking collectives, shards(): lax.all_to_all(attended, 'grp', split_axis=1, concat_axis=2, tiled=True)[0]  9.1 us
    sub x1, other arithmetic, attend_block(): weights = jnp.exp(scores - row_max)  7.51 us
  transfers between devices with their start and end apart: 4, of which 3 were waited for; matrix products, arithmetic and copies ran while one was open for 17% of the time, Pallas kernels for 0%

commit v1 on v0

--- a/solution.py
+++ b/solution.py
@@ -103,7 +103,12 @@
     prefix_len = prefix_cache.shape[1]
     slot_width = 2 * inner
     local_slot = prefix_cache.reshape(prefix_len, slot_width)
-    gathered = lax.all_gather(local_slot[None], "blk", axis=0, tiled=True)
+    ring = [local_slot[None]]
+    for hop in range(7):
+        ring.append(lax.ppermute(ring[-1], "blk", [(dev, (dev + 1) % 8) for dev in range(8)]))
+    gathered = jnp.roll(
+        jnp.concatenate(ring[::-1], axis=0), (lax.axis_index("blk") + 1) * ring[0].shape[0], axis=0
+    )
     prefix_rows = jnp.take(gathered, my_cols, axis=0)
     prefix_rows = prefix_rows.reshape(requests_col * prefix_len, 2, heads_dev, head_dim)
     key_rows = jnp.concatenate([prefix_rows[:, 0], projected[:, 1]], axis=0)

time: 209 us -> 224 us (1.072)
  local copies, waits for them, and re-layouts: 21.6 us -> 28.9 us
  waiting for transfers between devices: 75.7 us -> 79.8 us
  starting transfers between devices: 0.16 us -> 3.18 us
    ppermute x0 -> x7, waiting for transfers between devices: none -> 41.6 us  [shards(): lax.ppermute(ring[-1], 'blk', [(dev, (dev + 1) % 8) for dev in range(8)])]
    all_gather x1 -> x0, waiting for transfers between devices: 37 us -> none  [shards(): gathered = lax.all_gather(local_slot[None], 'blk', axis=0, tiled=True)]
    unnamed x15 -> x44, local copies, waits for them, and re-layouts: 3.57 us -> 12.4 us
    ppermute x0 -> x7, starting transfers between devices: none -> 3.06 us  [shards(): lax.ppermute(ring[-1], 'blk', [(dev, (dev + 1) % 8) for dev in range(8)])]
    slice x2, local copies, waits for them, and re-layouts: 3.47 us -> 0.91 us  [attend_block(): rel_bias[bucket_id][:, None, None]]
  transfers between devices with their start and end apart: 4 -> 10, of which waited for: 3 -> 8; matrix products, arithmetic and copies ran while one was open for 17% -> 15% of each run, Pallas kernels for 0% -> 0%
where the time goes in v1:
time: 224 us; the launch traced here: 223 us
  waiting for transfers between devices  79.8 us (36%)
  matrix products  51.5 us (23%)
  other arithmetic  36.4 us (16%)
  local copies, waits for them, and re-layouts  28.9 us (13%)
  between operations  14.1 us (6%)
  blocking collectives  9.1 us (4%)
  starting transfers between devices  3.18 us (1%)
    ppermute x7, waiting for transfers between devices, shards(): lax.ppermute(ring[-1], 'blk', [(dev, (dev + 1) % 8) for dev in range(8)])  41.6 us
    dot_general x1, matrix products, attend_block(): jnp.einsum('qhd,khd->hqk', queries, key_rows, preferred_element_type=jnp....  29.9 us
    reduce_scatter x1, waiting for transfers between devices, shards(): lax.psum_scatter(jnp.dot(activated, out_weight, preferred_element_type=jn...  24.2 us
    eq x1, other arithmetic, attend_block(): bucket == bucket_id  17.3 us
    all_gather x1, waiting for transfers between devices, shards(): lax.all_gather(normed_mlp, 'grp', axis=0, tiled=True)  13.9 us
    unnamed x44, local copies, waits for them, and re-layouts  12.4 us
    dot_general x1, matrix products, attend_block(): jnp.einsum('hqk,khd->qhd', weights, value_rows, preferred_element_type=jn...  10.5 us
    all_to_all x1, blocking collectives, shards(): lax.all_to_all(attended, 'grp', split_axis=1, concat_axis=2, tiled=True)[0]  9.1 us
  transfers between devices with their start and end apart: 10, of which 8 were waited for; matrix products, arithmetic and copies ran while one was open for 15% of the time, Pallas kernels for 0%

profile of v1, /device:TPU:0, one launch (start us, length us, event | category | flops | bytes accessed | tf_op | source)
XLA Modules:
  0.0 223.0 jit_solution(12961201421874763104)
XLA Ops:
  8.5 3.0 %collective-permute-start = (bf16[1,256,512]{2,1,0:T(8,128)(2,1)S(1)}, bf16[1,256,512]{2,1,0:T(8,128)(2,1)S(1)}, u32[]{:S(2)}, u32[]{:S(2)}) collective-permute-start(bf16[1,256,512]{2,1,0:T(8,128)(2,1)S(1)} %copy.52), channel_id=1, source_target_pairs={{0,1},{1,2},{2,3},{3,4},{4,5},{5,6},{6,7},{7,0},{8,9},{9,10},{10,1... | collective-permute-start | bytes 786440 | tf_op jit(solution)/shard_map/ppermute | solution.py:108
  12.5 1.8 fusion.13
  18.0 2.8 %collective-permute-done = bf16[1,256,512]{2,1,0:T(8,128)(2,1)S(1)} collective-permute-done((bf16[1,256,512]{2,1,0:T(8,128)(2,1)S(1)}, bf16[1,256,512]{2,1,0:T(8,128)(2,1)S(1)}, u32[]{:S(2)}, u32[]{:S(2)}) %collective-permute-start) | collective-permute-done | bytes 262176 | tf_op jit(solution)/shard_map/ppermute | solution.py:108
  21.0 10.0 %collective-permute-done.1 = bf16[1,256,512]{2,1,0:T(8,128)(2,1)S(1)} collective-permute-done((bf16[1,256,512]{2,1,0:T(8,128)(2,1)S(1)}, bf16[1,256,512]{2,1,0:T(8,128)(2,1)S(1)}, u32[]{:S(2)}, u32[]{:S(2)}) %collective-permute-start.1) | collective-permute-done | bytes 262176 | tf_op jit(solution)/shard_map/ppermute | solution.py:108
  31.0 17.3 %broadcast_compare_fusion.25 = (pred[512,1024]{1,0:T(8,128)(4,1)}, pred[512,1024]{1,0:T(8,128)(4,1)}, pred[512,1024]{1,0:T(8,128)(4,1)}, pred[512,1024]{1,0:T(8,...) fusion(s32[512]{0:T(512)S(1)} %add.912, ...), kind=kLoop, calls=%fused_computation.47 | loop fusion | flops 31981568 | bytes 16783360 | tf_op jit(solution)/shard_map/while/body/eval_jaxpr/eq | solution.py:50
  49.3 8.3 %collective-permute-done.3 = bf16[1,256,512]{2,1,0:T(8,128)(2,1)S(1)} collective-permute-done((bf16[1,256,512]{2,1,0:T(8,128)(2,1)S(1)}, bf16[1,256,512]{2,1,0:T(8,128)(2,1)S(1)}, u32[]{:S(2)}, u32[]{:S(2)}) %collective-permute-start.3) | collective-permute-done | bytes 262176 | tf_op jit(solution)/shard_map/ppermute | solution.py:108
  57.8 9.0 %collective-permute-done.4 = bf16[1,256,512]{2,1,0:T(8,128)(2,1)} collective-permute-done((bf16[1,256,512]{2,1,0:T(8,128)(2,1)S(1)}, bf16[1,256,512]{2,1,0:T(8,128)(2,1)}, u32[]{:S(2)}, u32[]{:S(2)}) %collective-permute-start.4) | collective-permute-done | bytes 262176 | tf_op jit(solution)/shard_map/ppermute | solution.py:108
  68.1 8.1 %collective-permute-done.5 = bf16[1,256,512]{2,1,0:T(8,128)(2,1)} collective-permute-done((bf16[1,256,512]{2,1,0:T(8,128)(2,1)}, bf16[1,256,512]{2,1,0:T(8,128)(2,1)}, u32[]{:S(2)}, u32[]{:S(2)}) %collective-permute-start.5) | collective-permute-done | bytes 262176 | tf_op jit(solution)/shard_map/ppermute | solution.py:108
  76.2 3.7 %convolution_convert_fusion.1 = bf16[512,768]{1,0:T(8,128)(2,1)} fusion(bf16[512,1024]{1,0:T(8,128)(2,1)} %all-gather.3.cloned.1.call-done, bf16[1024,768]{0,1:T(8,128)(2,1)} %bitcast.76), kind=kOutput, calls=%fused_computation.19 | convolution fusion | flops 805699584 | bytes 3407872 | tf_op jit(solution)/shard_map/dot_general | solution.py:84
  79.9 1.4 copy.56
  82.2 3.4 %collective-permute-done.6 = bf16[1,256,512]{2,1,0:T(8,128)(2,1)} collective-permute-done((bf16[1,256,512]{2,1,0:T(8,128)(2,1)}, bf16[1,256,512]{2,1,0:T(8,128)(2,1)}, u32[]{:S(2)}, u32[]{:S(2)}) %collective-permute-start.6) | collective-permute-done | bytes 262176 | tf_op jit(solution)/shard_map/ppermute | solution.py:108
  94.6 1.6 constant_dynamic-slice_fusion.2
  96.1 2.2 gather_fusion
  100.9 29.9 %add_select_fusion = f32[4,512,1024]{2,1,0:T(8,128)} fusion(f32[4]{0:T(128)S(1)} %get-tuple-element.62, f32[4]{0:T(128)S(1)} %get-tuple-element.63, f32[4]{0:T(128)S(1)} %get-tuple-element.23, f32[4]{0:T(128)S(1)} %get-tuple-element.24, f32[4]{0:T(128)S(1)} %get-tuple-element.25, f32[4]{0:T(128)S(1)} %get-tuple-element.26, f32[4]{0:T(128)S(1)} %get-tuple-element.27, ...), kind=kOutput, calls=%fused_computation.4 | convolution fusion | flops 340787200 | bytes 26492928 | tf_op jit(solution)/shard_map/while/body/eval_jaxpr/qhd,khd->hqk/dot_general | solution.py:45
  130.8 7.5 %fusion.30 = f32[4,512]{1,0:T(4,128)S(1)} fusion(f32[4,512,1024]{2,1,0:T(8,128)} %add_select_fusion), kind=kOutput, calls=%fused_computation.155 | output fusion | flops 4195327 | bytes 8396800 | tf_op jit(solution)/shard_map/while/body/eval_jaxpr/sub | solution.py:55
  138.4 10.5 %fusion.10 = bf16[4,64,512]{2,1,0:T(8,128)(2,1)} fusion(f32[4,512]{1,0:T(4,128)S(1)} %fusion.30, bf16[512,4,64]{0,2,1:T(8,128)(2,1)S(1)} %copy-done.8, bf16[512,4,64]{0,2,1:T(8,128)(2,1)S(1)} %get-tuple-element.66, f32[4,512,1024]{2,1,0:T(8,128)} %add_select_fusion), kind=kOutput, calls=%fused_computation.21 | convolution fusion | flops 275909632 | bytes 9183232 | tf_op jit(solution)/shard_map/while/body/eval_jaxpr/hqk,khd->qhd/dot_general | solution.py:57
  150.7 2.9 %reduce.67 = bf16[512,256]{1,0:T(8,128)(2,1)} reduce(bf16[512,1,256]{2,1,0:T(2,128)(2,1)S(1)} %bitcast.69, bf16[]{:T(256)} %broadcast.2961), dimensions={1}, to_apply=%bitcast.52.reduce_sub_computation | reduce | bytes 524290
  154.6 9.1 %all_to_all.15 = bf16[4,2,16384]{2,1,0:T(2,128)(2,1)} all-to-all(bf16[4,2,16384]{2,1,0:T(2,128)(2,1)S(1)} %reshape.1101), channel_id=1, replica_groups=mesh['grp'=4,'blk'=8] {'grp'}, dimensions={0} | all-to-all | bytes 524288 | tf_op jit(solution)/shard_map/all_to_all | solution.py:142
  165.6 1.8 copy.59
  167.4 2.2 multiply_reduce_fusion
  170.5 13.9 %all-gather.5.cloned.1.call-done = bf16[512,1024]{1,0:T(8,128)(2,1)} async-done(((bf16[128,1024]{1,0:T(8,128)(2,1)}), bf16[512,1024]{1,0:T(8,128)(2,1)}) %all-gather.5.cloned.1.call-update) | async-done | bytes 1048592 | tf_op jit(solution)/shard_map/all_gather | solution.py:147
  184.4 5.2 %convolution_convert_fusion = bf16[512,1024]{1,0:T(8,128)(2,1)} fusion(bf16[1024,1024]{1,0:T(8,128)(2,1)S(1)} %copy-done, bf16[512,1024]{1,0:T(8,128)(2,1)} %all-gather.5.cloned.1.call-done, bf16[1024,1024]{1,0:T(8,128)(2,1)} %param.24), kind=kOutput, calls=%fused_computation.18 | convolution fusion | flops 2149056512 | bytes 6291456 | tf_op jit(solution)/shard_map/dot_general | solution.py:153
  190.5 24.2 %reduce-scatter.2.cloned.1.call-done = bf16[128,1024]{1,0:T(8,128)(2,1)} async-done(((bf16[512,1024]{1,0:T(8,128)(2,1)}), bf16[128,1024]{1,0:T(8,128)(2,1)}) %reduce-scatter.2.cloned.1.call-update) | async-done | bytes 262160 | tf_op jit(solution)/shard_map/reduce_scatter | solution.py:152
  214.8 1.7 fusion.20
  (93 shorter events, 27.4 us)
Async XLA Ops:
  7.2 177.3 %copy-start = (bf16[1024,1024]{1,0:T(8,128)(2,1)S(1)}, bf16[1024,1024]{1,0:T(8,128)(2,1)}, u32[]{:S(2)}) copy-start(bf16[1024,1024]{1,0:T(8,128)(2,1)} %param.25) | copy-start | bytes 6291460
  7.2 69.0 %all-gather.3.cloned.1.call-start = ((), (), s32[]{:S(2)}) async-start(), calls=%async_computation.2 | async-start | bytes 1310720 | tf_op jit(solution)/shard_map/all_gather | solution.py:85
  8.5 12.3 %collective-permute-start = (bf16[1,256,512]{2,1,0:T(8,128)(2,1)S(1)}, bf16[1,256,512]{2,1,0:T(8,128)(2,1)S(1)}, u32[]{:S(2)}, u32[]{:S(2)}) collective-permute-start(bf16[1,256,512]{2,1,0:T(8,128)(2,1)S(1)} %copy.52), channel_id=1, source_target_pairs={{0,1},{1,2},{2,3},{3,4},{4,5},{5,6},{6,7},{7,0},{8,9},{9,10},{10,1... | collective-permute-start | bytes 786440 | tf_op jit(solution)/shard_map/ppermute | solution.py:108
  14.4 170.1 %all-gather.5.cloned.1.call-start = ((), (), s32[]{:S(2)}) async-start(), calls=%async_computation.3 | async-start | bytes 1310720 | tf_op jit(solution)/shard_map/all_gather | solution.py:147
  20.8 10.2 %collective-permute-start.1 = (bf16[1,256,512]{2,1,0:T(8,128)(2,1)S(1)}, bf16[1,256,512]{2,1,0:T(8,128)(2,1)S(1)}, u32[]{:S(2)}, u32[]{:S(2)}) collective-permute-start(bf16[1,256,512]{2,1,0:T(8,128)(2,1)S(1)} %collective-permute-done), channel_id=1, source_target_pairs={{0,1},{1,2},{2,3},{3,4},{4,5},{5,6},{6,7},{7,0},{8,9},{9,10},{10,1... | collective-permute-start | bytes 786440 | tf_op jit(solution)/shard_map/ppermute | solution.py:108
  21.0 27.4 %copy-start.1 = (f32[32,4]{0,1:T(4,128)S(1)}, f32[32,4]{0,1:T(4,128)}, u32[]{:S(2)}) copy-start(f32[32,4]{0,1:T(4,128)} %param.16) | copy-start | bytes 1540
  31.0 17.3 %copy-start.2 = (bf16[1,256,512]{2,1,0:T(8,128)(2,1)}, bf16[1,256,512]{2,1,0:T(8,128)(2,1)S(1)}, u32[]{:S(2)}) copy-start(bf16[1,256,512]{2,1,0:T(8,128)(2,1)S(1)} %collective-permute-done.1) | copy-start | bytes 786436
  31.0 17.3 %collective-permute-start.2 = (bf16[1,256,512]{2,1,0:T(8,128)(2,1)S(1)}, bf16[1,256,512]{2,1,0:T(8,128)(2,1)S(1)}, u32[]{:S(2)}, u32[]{:S(2)}) collective-permute-start(bf16[1,256,512]{2,1,0:T(8,128)(2,1)S(1)} %collective-permute-done.1), channel_id=1, source_target_pairs={{0,1},{1,2},{2,3},{3,4},{4,5},{5,6},{6,7},{7,0},{8,9},{9,10},{10,1... | collective-permute-start | bytes 786440 | tf_op jit(solution)/shard_map/ppermute | solution.py:108
  48.3 27.9 %copy-start.4 = (bf16[1,256,512]{2,1,0:T(8,128)(2,1)}, bf16[1,256,512]{2,1,0:T(8,128)(2,1)S(1)}, u32[]{:S(2)}) copy-start(bf16[1,256,512]{2,1,0:T(8,128)(2,1)S(1)} %collective-permute-done.2) | copy-start | bytes 786436
  48.3 9.3 %collective-permute-start.3 = (bf16[1,256,512]{2,1,0:T(8,128)(2,1)S(1)}, bf16[1,256,512]{2,1,0:T(8,128)(2,1)S(1)}, u32[]{:S(2)}, u32[]{:S(2)}) collective-permute-start(bf16[1,256,512]{2,1,0:T(8,128)(2,1)S(1)} %collective-permute-done.2), channel_id=1, source_target_pairs={{0,1},{1,2},{2,3},{3,4},{4,5},{5,6},{6,7},{7,0},{8,9},{9,10},{10,1... | collective-permute-start | bytes 786440 | tf_op jit(solution)/shard_map/ppermute | solution.py:108
  57.6 18.6 %copy-start.6 = (bf16[1,256,512]{2,1,0:T(8,128)(2,1)}, bf16[1,256,512]{2,1,0:T(8,128)(2,1)S(1)}, u32[]{:S(2)}) copy-start(bf16[1,256,512]{2,1,0:T(8,128)(2,1)S(1)} %collective-permute-done.3) | copy-start | bytes 786436
  57.6 9.2 %collective-permute-start.4 = (bf16[1,256,512]{2,1,0:T(8,128)(2,1)S(1)}, bf16[1,256,512]{2,1,0:T(8,128)(2,1)}, u32[]{:S(2)}, u32[]{:S(2)}) collective-permute-start(bf16[1,256,512]{2,1,0:T(8,128)(2,1)S(1)} %collective-permute-done.3), channel_id=1, source_target_pairs={{0,1},{1,2},{2,3},{3,4},{4,5},{5,6},{6,7},{7,0},{8,9},{9,10},{10,1... | collective-permute-start | bytes 786440 | tf_op jit(solution)/shard_map/ppermute | solution.py:108
  66.8 9.4 %collective-permute-start.5 = (bf16[1,256,512]{2,1,0:T(8,128)(2,1)}, bf16[1,256,512]{2,1,0:T(8,128)(2,1)}, u32[]{:S(2)}, u32[]{:S(2)}) collective-permute-start(bf16[1,256,512]{2,1,0:T(8,128)(2,1)} %collective-permute-done.4), channel_id=1, source_target_pairs={{0,1},{1,2},{2,3},{3,4},{4,5},{5,6},{6,7},{7,0},{8,9},{9,10},{10,1... | collective-permute-start | bytes 786440 | tf_op jit(solution)/shard_map/ppermute | solution.py:108
  76.2 9.4 %collective-permute-start.6 = (bf16[1,256,512]{2,1,0:T(8,128)(2,1)}, bf16[1,256,512]{2,1,0:T(8,128)(2,1)}, u32[]{:S(2)}, u32[]{:S(2)}) collective-permute-start(bf16[1,256,512]{2,1,0:T(8,128)(2,1)} %collective-permute-done.5), channel_id=1, source_target_pairs={{0,1},{1,2},{2,3},{3,4},{4,5},{5,6},{6,7},{7,0},{8,9},{9,10},{10,1... | collective-permute-start | bytes 786440 | tf_op jit(solution)/shard_map/ppermute | solution.py:108
  81.3 13.1 %copy-start.7 = (bf16[1,256,512]{2,1,0:T(8,128)(2,1)S(1)}, bf16[1,256,512]{2,1,0:T(8,128)(2,1)}, u32[]{:S(2)}) copy-start(bf16[1,256,512]{2,1,0:T(8,128)(2,1)} %copy-done.6) | copy-start | bytes 786436
  81.3 13.1 %copy-start.5 = (bf16[1,256,512]{2,1,0:T(8,128)(2,1)S(1)}, bf16[1,256,512]{2,1,0:T(8,128)(2,1)}, u32[]{:S(2)}) copy-start(bf16[1,256,512]{2,1,0:T(8,128)(2,1)} %copy-done.4) | copy-start | bytes 786436
  81.3 13.1 %copy-start.3 = (bf16[1,256,512]{2,1,0:T(8,128)(2,1)S(1)}, bf16[1,256,512]{2,1,0:T(8,128)(2,1)}, u32[]{:S(2)}) copy-start(bf16[1,256,512]{2,1,0:T(8,128)(2,1)} %copy-done.2) | copy-start | bytes 786436
  130.8 7.5 %copy-start.8 = (bf16[512,4,64]{0,2,1:T(8,128)(2,1)S(1)}, bf16[512,4,64]{0,2,1:T(8,128)(2,1)}, u32[]{:S(2)}) copy-start(bf16[512,4,64]{0,2,1:T(8,128)(2,1)} %get-tuple-element.64) | copy-start | bytes 786436
  148.9 20.8 %copy-start.9 = (f32[1024]{0:T(1024)S(1)}, f32[1024]{0:T(1024)}, u32[]{:S(2)}) copy-start(f32[1024]{0:T(1024)} %param.23) | copy-start | bytes 12292
  170.5 44.3 %reduce-scatter.2.cloned.1.call-start = ((), (), s32[]{:S(2)}) async-start(), calls=%async_computation.4 | async-start | bytes 1310720 | tf_op jit(solution)/shard_map/reduce_scatter | solution.py:152
Sparse Core Ops, SparseCore 0:
  14.5 17.0 all-gather.2
  170.6 13.7 all-gather.4
  189.8 24.8 reduce-scatter.1
